TPU v7x, 32 devices: a whole 2x2x4 slice. The times are simulated.
32 devices in a mesh: freq: 2 (over x), row: 4 (over y, core), blk: 4 (over z).
Axes of the slice: x: 2, y: 2, z: 4, core: 2. Of those that a mesh axis runs over, the one named last changes fastest.
Arguments:
- counts: int32 [8192, 8, 128], P(('freq', 'row', 'blk')), parts along dimension 0, may hold values from 0 to 28, as said below
- subspace: bfloat16 [8192, 32], P(('freq', 'row', 'blk')), parts along dimension 0, may hold values from -6 to 6
Outputs:
- modes: float32 [8192, 32], P(('freq', 'row', 'blk')), parts along dimension 0
There are 2 independent parts, one for each index of `freq`. A program takes and returns all parts, laid end to end along the dimension named above; each array names one. Nothing has to cross between parts.
Inputs may be any that keep to these rules, and one draw needn't show every extreme that they name: Integer spike counts.
All inputs are finite; a program needn't handle non-finite values.
Results may differ from a plain program's by a relative error of at most 0.008.
Values may be sent and summed in bfloat16 or wider, within the bound.
A program may use at most 64 MiB of HBM per device.

v0:
```python
import math

import jax
import jax.numpy as jnp
from jax import lax
from jax.sharding import PartitionSpec as P

SEGS = 8
TAPERS = 8
EPOCH_STEPS = 128
SPECTRAL_SLOT = 9
MODES = 32


def spectral_table():
    clock_moments = jnp.arange(EPOCH_STEPS, dtype=jnp.float32)
    window_degrees = jnp.arange(TAPERS, dtype=jnp.float32) + 1.0
    prolate_windows = jnp.sqrt(2.0 / (EPOCH_STEPS + 1.0)) * jnp.sin(
        jnp.pi * (clock_moments[:, None] + 1.0) * window_degrees[None, :] / (EPOCH_STEPS + 1.0)
    )
    oscillation_radians = 2.0 * jnp.pi * SPECTRAL_SLOT * clock_moments / EPOCH_STEPS
    return jnp.concatenate(
        [
            prolate_windows * jnp.cos(oscillation_radians)[:, None],
            -prolate_windows * jnp.sin(oscillation_radians)[:, None],
        ],
        axis=1,
    )


def make_spectra(counts):
    values = counts.astype(jnp.float32)
    centered = values - jnp.mean(values, axis=2, keepdims=True)
    height = counts.shape[0]
    flattened = centered.reshape(height * SEGS, EPOCH_STEPS)
    result = jnp.dot(
        flattened,
        spectral_table(),
        precision=lax.Precision.HIGHEST,
        preferred_element_type=jnp.float32,
    )
    return result.reshape(height, SEGS * 2 * TAPERS).astype(jnp.bfloat16)


def twist(spectra):
    height = spectra.shape[0]
    pieces_view = spectra.reshape(height, SEGS, 2, TAPERS)
    return jnp.stack([pieces_view[:, :, 1], -pieces_view[:, :, 0]], axis=2).reshape(
        height, SEGS * 2 * TAPERS
    )


def inverse_power(spectra):
    widened = spectra.astype(jnp.float32)
    return 1.0 / (jnp.sum(widened * widened, axis=1) + 1e-05)


def tile_image(stacked, inverse_rows, column_spectra, inverse_cols, column_subspace):
    height = inverse_rows.shape[0]
    products = lax.dot_general(
        stacked, column_spectra, (((1,), (1,)), ((), ())), preferred_element_type=jnp.float32
    )
    real_part = products[:height]
    imag_part = products[height:]
    squared = (
        (real_part * real_part + imag_part * imag_part)
        * inverse_rows[:, None]
        * inverse_cols[None, :]
    )
    degrees = float(SEGS * TAPERS)
    coherence = jnp.maximum((degrees * squared - 1.0) / (degrees - 1.0), 0.0).astype(jnp.bfloat16)
    return jnp.dot(coherence, column_subspace, preferred_element_type=jnp.float32)


def fold_pieces(accumulated, stacked, inverse_rows, pieces):
    column_spectra, column_subspace = pieces
    row_count = column_spectra.shape[0]
    rows_per_block = math.gcd(row_count, 2048)
    turns = row_count // rows_per_block

    def add_block(position, running):
        offset = position * rows_per_block
        spectra_here = lax.dynamic_slice_in_dim(column_spectra, offset, rows_per_block, 0)
        subspace_here = lax.dynamic_slice_in_dim(column_subspace, offset, rows_per_block, 0)
        return running + tile_image(
            stacked, inverse_rows, spectra_here, inverse_power(spectra_here), subspace_here
        )

    return lax.fori_loop(0, turns, add_block, accumulated)


def local(counts, subspace):
    spectra = make_spectra(counts)
    own_inverse = inverse_power(spectra)
    spectra_group, krylov_cluster = (
        lax.all_gather(spectra, "row", axis=0, tiled=True),
        lax.all_gather(subspace, "row", axis=0, tiled=True),
    )
    stacked = jnp.concatenate([spectra, twist(spectra)], axis=0)
    starting = jnp.zeros((spectra.shape[0], MODES), jnp.float32)
    projected = fold_pieces(
        starting,
        stacked,
        own_inverse,
        (
            lax.all_gather(spectra_group, "blk", axis=0, tiled=True),
            lax.all_gather(krylov_cluster, "blk", axis=0, tiled=True),
        ),
    )
    local_gram = jnp.dot(
        projected.T, projected, precision=lax.Precision.HIGHEST, preferred_element_type=jnp.float32
    )
    gram = lax.psum(local_gram, ("row", "blk"))
    factor = jnp.linalg.cholesky(gram)
    solved = jax.scipy.linalg.solve_triangular(factor, projected.T, lower=True)
    neuron_total = counts.shape[0] * lax.axis_size("row") * lax.axis_size("blk")
    return solved.T * jnp.sqrt(jnp.float32(neuron_total))


def solution(mesh):
    return jax.shard_map(
        local,
        mesh=mesh,
        in_specs=(P(("freq", "row", "blk"), None, None), P(("freq", "row", "blk"), None)),
        out_specs=P(("freq", "row", "blk"), None),
        check_vma=False,
    )
```

profile of v0, /device:TPU:0, one launch (start us, length us, event | category | flops | bytes accessed | tf_op | source)
XLA Modules:
  0.0 148.0 jit_solution(811683290244548175)
XLA Ops:
  6.6 1.6 %convert_reduce_fusion = f32[256,8]{1,0:T(8,128)S(1)} fusion(s32[256,8,128]{2,1,0:T(8,128)} %param.4), kind=kLoop, calls=%fused_computation.27 | loop fusion | flops 522240 | bytes 1056768 | tf_op jit(solution)/shard_map/reduce_sum | solution.py:33
  8.2 0.1 fusion.27
  8.3 2.4 %multiply_reduce_fusion.1 = (f32[2048]{0:T(1024)S(1)}, bf16[2048,16]{0,1:T(8,128)(2,1)S(1)}) fusion(f32[128,8]{0,1:T(8,128)S(1)} %get-tuple-element.196, f32[128,8]{0,1:T(8,128)S(1)} %get-tuple-element.195, s32[256,8,128]{2,1,0:T(8,128)} %param.4, f32[256,8]{1,0:T(8,128)S(1)} %broadcast_multiply_fusion), kind=kOutput, calls=%fused_computation.30 | convolution fusion | flops 50987008 | bytes 1138688 | tf_op jit(solution)/shard_map/dot_general | solution.py:36
  10.7 0.3 copy.20
  11.0 0.3 convert_element_type.40
  11.4 7.7 %all_gather.12 = bf16[1024,128]{1,0:T(8,128)(2,1)} all-gather(bf16[256,128]{1,0:T(8,128)(2,1)S(1)} %convert_element_type.40), channel_id=1, replica_groups=mesh['freq'=2,'row'=4,'blk'=4] {'row'}, dimensions={0}, use_global_device_ids=true | all-gather | bytes 327680 | tf_op jit(solution)/shard_map/all_gather | solution.py:96
  19.1 1.2 convert_element_type.41
  20.3 0.1 copy.24
  20.4 0.1 reduce_sum.43
  20.5 0.1 fusion.30
  20.6 0.2 copy.22
  20.8 0.2 copy.28
  21.0 0.1 copy.23
  21.2 0.1 reduce_sum.44
  21.3 5.9 %all_gather.14 = bf16[1024,32]{1,0:T(8,128)(2,1)S(1)} all-gather(bf16[256,32]{1,0:T(8,128)(2,1)S(1)} %copy.24), channel_id=1, replica_groups=mesh['freq'=2,'row'=4,'blk'=4] {'row'}, dimensions={0}, use_global_device_ids=true | all-gather | bytes 81920 | tf_op jit(solution)/shard_map/all_gather | solution.py:97
  27.1 38.0 %all_gather.15 = bf16[4096,32]{1,0:T(8,128)(2,1)S(1)} all-gather(bf16[1024,32]{1,0:T(8,128)(2,1)S(1)} %all_gather.14), channel_id=1, replica_groups=mesh['freq'=2,'row'=4,'blk'=4] {'blk'}, dimensions={0}, use_global_device_ids=true | all-gather | bytes 327680 | tf_op jit(solution)/shard_map/all_gather | solution.py:107
  65.2 0.3 all-gather.2.cloned.1.call-done
  65.5 8.3 %while.16 = (s32[]{:T(128)}, f32[256,32]{0,1:T(8,128)S(1)}, bf16[4096,128]{1,0:T(8,128)(2,1)}, bf16[512,128]{1,0:T(8,128)(2,1)S(1)}, f32[256]{0:T(256)S(1)}, /*i...) while((s32[]{:T(128)}, f32[256,32]{0,1:T(8,128)S(1)}, ...), condition=%wide.region_5.0_spmd.clone, body=%wide.region_3.5_spmd.clone.sunk | while | flops 308037632 | bytes 10192049 | solution.py:89
  65.5 1.4 multiply_reduce_fusion.3
  66.9 1.8 %convolution_bitcast_fusion.2 = f32[512,2048]{0,1:T(8,128)S(1)} fusion(bf16[512,128]{1,0:T(8,128)(2,1)S(1)} %get-tuple-element.261, bf16[4096,128]{1,0:T(8,128)(2,1)} %get-tuple-element.260, s32[]{:T(128)S(6)} %select_n.21), kind=kOutput, calls=%fused_computation.clone.1 | convolution fusion | flops 268435456 | bytes 4849668 | tf_op jit(solution)/shard_map/while/body/eval_jaxpr/dot_general | solution.py:60
  68.6 0.9 convolution_add_fusion.2
  69.6 1.4 multiply_reduce_fusion.3
  71.0 1.8 %convolution_bitcast_fusion.2 = f32[512,2048]{0,1:T(8,128)S(1)} fusion(bf16[512,128]{1,0:T(8,128)(2,1)S(1)} %get-tuple-element.261, bf16[4096,128]{1,0:T(8,128)(2,1)} %get-tuple-element.260, s32[]{:T(128)S(6)} %select_n.21), kind=kOutput, calls=%fused_computation.clone.1 | convolution fusion | flops 268435456 | bytes 4849668 | tf_op jit(solution)/shard_map/while/body/eval_jaxpr/dot_general | solution.py:60
  72.8 0.9 convolution_add_fusion.2
  73.7 0.2 fusion.31
  73.9 59.6 %psum.7 = f32[32,32]{0,1:T(8,128)S(1)} all-reduce(f32[32,32]{0,1:T(8,128)S(1)} %fusion.31), channel_id=1, replica_groups=mesh['freq'=2,'row'=4,'blk'=4] {'row','blk'}, use_global_device_ids=true, to_apply=%region_6.7 | all-reduce | flops 1024 | bytes 8192 | tf_op jit(solution)/shard_map/psum | solution.py:113
  133.5 0.1 copy.26
  133.6 2.9 %cholesky.16 = f32[32,32]{1,0:T(8,128)S(1)} custom-call(f32[32,32]{1,0:T(8,128)S(1)} %fusion.23), custom_call_target="Cholesky" | custom-call | tf_op jit(solution)/shard_map/jit(cholesky)/cholesky | solution.py:114
  136.6 0.6 compare_reduce_fusion
  137.2 0.7 fusion.21
  137.9 2.4 %custom-call.7 = f32[1,32,32]{1,2,0:T(8,128)S(1)} custom-call(f32[1,32,32]{2,1,0:T(8,128)S(1)} %fusion.21), custom_call_target="InvertDiagBlocksLowerTriangular" | custom-call | tf_op jit(solution)/shard_map/jit(_solve_triangular)/triangular_solve | solution.py:115
  140.3 0.9 convolution_multiply_fusion
  (17 shorter events, 0.2 us)
Async XLA Ops:
  6.5 58.9 %all-gather.2.cloned.1.call-start = ((), (), s32[]{:S(2)}) async-start(), calls=%async_computation | async-start | bytes 1310720 | tf_op jit(solution)/shard_map/all_gather | solution.py:106
  8.3 12.0 %copy-start = (bf16[256,32]{0,1:T(8,128)(2,1)S(1)}, bf16[256,32]{0,1:T(8,128)(2,1)}, u32[]{:S(2)}) copy-start(bf16[256,32]{0,1:T(8,128)(2,1)} %param.5) | copy-start | bytes 49156
Sparse Core Ops, SparseCore 0:
  19.2 46.2 all-gather.1
where the time goes:
time: 148 us
  blocking collectives  111 us (75%)
  between operations  13.6 us (9%)
  other arithmetic  11.4 us (8%)
  matrix products  8.82 us (6%)
  local copies, waits for them, and re-layouts  2.69 us (2%)
    psum x1, blocking collectives, local(): gram = lax.psum(local_gram, ('row', 'blk'))  59.6 us
    all_gather x1, blocking collectives, local(): lax.all_gather(krylov_cluster, 'blk', axis=0, tiled=True)  38 us
    all_gather x1, blocking collectives, local(): lax.all_gather(spectra, 'row', axis=0, tiled=True)  7.67 us
    all_gather x1, blocking collectives, local(): lax.all_gather(subspace, 'row', axis=0, tiled=True)  5.86 us
    another operation x3, other arithmetic, local(): factor = jnp.linalg.cholesky(gram)  3.59 us
    dot_general x2, matrix products, tile_image(): lax.dot_general(stacked, column_spectra, (((1,), (1,)), ((), ())), prefer...  3.51 us
    another operation x2, other arithmetic, local(): solved = jax.scipy.linalg.solve_triangular(factor, projected.T, lower=True)  3.09 us
  transfers between devices with their start and end apart: 1, of which 1 were waited for; matrix products, arithmetic and copies ran while one was open for 1% of the time, Pallas kernels for 0%

commit v1 on v0

v1 whole, which is shorter than its diff:
```python
import functools
import math

import jax
import jax.numpy as jnp
import ml_dtypes
import numpy as np
from jax import lax
from jax.experimental import pallas as pl
from jax.experimental.pallas import tpu as pltpu
from jax.sharding import PartitionSpec as P

SEGS = 8
TAPERS = 8
EPOCH_STEPS = 128
SPECTRAL_SLOT = 9
MODES = 32
WIDTH = SEGS * 2 * TAPERS
MESH = pl.DeviceIdType.MESH


def centred_table():
    t = np.arange(EPOCH_STEPS, dtype=np.float64)
    k = np.arange(TAPERS, dtype=np.float64) + 1.0
    h = np.sqrt(2.0 / (EPOCH_STEPS + 1.0)) * np.sin(
        np.pi * (t[:, None] + 1.0) * k[None, :] / (EPOCH_STEPS + 1.0)
    )
    angle = 2.0 * np.pi * SPECTRAL_SLOT * t / EPOCH_STEPS
    table = np.concatenate([h * np.cos(angle)[:, None], -h * np.sin(angle)[:, None]], axis=1)
    return table - table.mean(axis=0, keepdims=True)


def split_table():
    table = centred_table()
    whole = np.zeros((SEGS * EPOCH_STEPS, WIDTH))
    for s in range(SEGS):
        whole[s * EPOCH_STEPS : (s + 1) * EPOCH_STEPS, s * 2 * TAPERS : (s + 1) * 2 * TAPERS] = table
    pieces = []
    rest = whole
    for _ in range(3):
        piece = rest.astype(ml_dtypes.bfloat16)
        pieces.append(piece)
        rest = rest - piece.astype(np.float64)
    return np.concatenate(pieces, axis=1)


def twist_matrix():
    m = np.zeros((WIDTH, WIDTH), np.float32)
    for s in range(SEGS):
        for c in range(TAPERS):
            re, im = s * 2 * TAPERS + c, s * 2 * TAPERS + TAPERS + c
            m[im, re] = 1.0
            m[re, im] = -1.0
    return m.astype(ml_dtypes.bfloat16)


def each(first, last, body):
    if last - first <= 16:
        for i in range(first, last):
            body(i)
    else:
        lax.fori_loop(first, last, lambda i, c: (body(i), c)[1], 0)


def nt(a, b, precision=None):
    return lax.dot_general(
        a, b, (((1,), (1,)), ((), ())), precision=precision, preferred_element_type=jnp.float32
    )


def kernel(
    nr, nb, counts, sub_t, table, twist, out,
    xs, tab, rows, twisted, irow, cols, subs, part, landed, grams,
    x_sem, t_sem, row_send, row_recv, col_send, col_recv, sub_send, sub_recv,
    part_send, part_recv, gram_send, gram_recv,
):
    my_row, my_blk = lax.axis_index("row"), lax.axis_index("blk")
    height = rows.shape[1]

    def peer(dr, db):
        return {"row": lax.rem(my_row + dr, nr), "blk": lax.rem(my_blk + db, nb)}

    loads = [pltpu.make_async_copy(counts.at[:, s], xs.at[s], x_sem.at[s]) for s in range(SEGS)]
    table_load = pltpu.make_async_copy(table, tab, t_sem)
    table_load.start()
    for load in loads:
        load.start()

    barrier = pltpu.get_barrier_semaphore()
    each(1, nr * nb, lambda k: pl.semaphore_signal(
        barrier, inc=1, device_id=peer(k // nb, k % nb), device_id_type=MESH))

    subs[0] = sub_t[...]
    table_load.wait()
    total = jnp.zeros((height, 3 * WIDTH), jnp.float32)
    for s in range(0, SEGS, 2):
        loads[s].wait()
        loads[s + 1].wait()
        x = jnp.concatenate([xs[s], xs[s + 1]], axis=1).astype(jnp.float32).astype(jnp.bfloat16)
        total += jnp.dot(
            x, tab[s * EPOCH_STEPS : (s + 2) * EPOCH_STEPS], preferred_element_type=jnp.float32
        )
    spectra = (total[:, 2 * WIDTH :] + total[:, WIDTH : 2 * WIDTH]) + total[:, :WIDTH]
    spectra = spectra.astype(jnp.bfloat16)
    rows[0] = spectra
    cols[0] = spectra

    pl.semaphore_wait(barrier, nr * nb - 1)

    def col_copy(d):
        return pltpu.make_async_remote_copy(
            src_ref=rows.at[0], dst_ref=cols.at[d], send_sem=col_send.at[d],
            recv_sem=col_recv.at[d], device_id=peer(0, d), device_id_type=MESH)

    def sub_copy(d):
        return pltpu.make_async_remote_copy(
            src_ref=subs.at[0], dst_ref=subs.at[d], send_sem=sub_send.at[d],
            recv_sem=sub_recv.at[d], device_id=peer(0, d), device_id_type=MESH)

    def row_copy(d):
        return pltpu.make_async_remote_copy(
            src_ref=rows.at[0], dst_ref=rows.at[d], send_sem=row_send.at[d],
            recv_sem=row_recv.at[d], device_id=peer(d, 0), device_id_type=MESH)

    def part_copy(d):
        return pltpu.make_async_remote_copy(
            src_ref=part.at[d], dst_ref=landed.at[d], send_sem=part_send.at[d],
            recv_sem=part_recv.at[d], device_id=peer(nr - d, 0), device_id_type=MESH)

    def gram_copy(k):
        return pltpu.make_async_remote_copy(
            src_ref=grams.at[0], dst_ref=grams.at[k], send_sem=gram_send.at[k],
            recv_sem=gram_recv.at[k], device_id=peer(k // nb, k % nb), device_id_type=MESH)

    each(1, nr, lambda d: row_copy(d).start())

    def send_cols(d):
        col_copy(d).start()
        sub_copy(d).start()

    each(1, nb, send_cols)

    degrees = float(SEGS * TAPERS)
    ones = jnp.ones((8, WIDTH), jnp.float32)

    def prepare_row(r):
        here = rows[r]
        twisted[r] = jnp.dot(here, twist[...], preferred_element_type=jnp.float32).astype(jnp.bfloat16)
        wide = here.astype(jnp.float32)
        power = nt(ones, wide * wide, lax.Precision.HIGHEST)
        irow[r] = (degrees / (degrees - 1.0)) / (power + 1e-05)

    def column(d):
        wide = cols[d].astype(jnp.float32)
        return 1.0 / (jnp.sum(wide * wide, axis=1, keepdims=True) + 1e-05)

    def tile(d, r, icol):
        here = cols[d]
        re = nt(here, rows[r])
        im = nt(here, twisted[r])
        msc = (re * re + im * im) * icol * irow[r, 0:1]
        coherence = jnp.maximum(msc - 1.0 / (degrees - 1.0), 0.0).astype(jnp.bfloat16)
        return jnp.dot(subs[d], coherence, preferred_element_type=jnp.float32)

    own = column(0)
    for r in range(nr):
        if r > 0:
            row_copy(r).wait()
        prepare_row(r)
        part[r] = tile(0, r, own)

    def add_column(d, final):
        col_copy(d).wait()
        sub_copy(d).wait()
        icol = column(d)
        for r in list(range(1, nr)) + [0]:
            part[r] += tile(d, r, icol)
            if final and r > 0:
                part_copy(r).start()

    each(1, nb - 1, lambda d: add_column(d, False))
    add_column(nb - 1, True)

    image = part[0]
    for r in range(1, nr):
        part_copy(r).wait()
        image += landed[r]

    gram = nt(image, image, lax.Precision.HIGHEST)
    quarter = MODES // 4
    grams[0] = jnp.concatenate([gram[q * quarter : (q + 1) * quarter] for q in range(4)], axis=1)
    each(1, nr * nb, lambda k: gram_copy(k).start())
    each(1, nr * nb, lambda k: gram_copy(k).wait())
    packed = jnp.sum(grams[...], axis=0)
    gram = jnp.concatenate([packed[:, q * MODES : (q + 1) * MODES] for q in range(4)], axis=0)

    sub_id = lax.broadcasted_iota(jnp.int32, (MODES, 2 * MODES), 0)
    lane_id = lax.broadcasted_iota(jnp.int32, (MODES, 2 * MODES), 1)
    eye = (sub_id == lane_id).astype(jnp.float32)
    work = jnp.concatenate([eye[:, :MODES], gram], axis=1)
    for k in range(MODES - 1):
        top = work[k : k + 1]
        pivot = work[k : k + 1, MODES + k : MODES + k + 1]
        below = work[:, MODES + k : MODES + k + 1]
        update = below * (top * (1.0 / pivot))
        work = work - jnp.where(sub_id > k, update, 0.0)
    pivots = jnp.sum(jnp.where(lane_id == sub_id + MODES, work, 0.0), axis=1, keepdims=True)
    neurons = float(height * nr * nb)
    inverse = work[:, :MODES] * (math.sqrt(neurons) / jnp.sqrt(pivots))
    out[...] = jnp.dot(
        inverse, image, precision=lax.Precision.HIGHEST, preferred_element_type=jnp.float32
    )


def local(nr, nb, counts, subspace):
    height = counts.shape[0]
    vmem = pl.BlockSpec(memory_space=pltpu.VMEM)
    hbm = pl.BlockSpec(memory_space=pl.ANY)
    dma = pltpu.SemaphoreType.DMA
    modes_t = pl.pallas_call(
        functools.partial(kernel, nr, nb),
        out_shape=jax.ShapeDtypeStruct((MODES, height), jnp.float32),
        in_specs=[hbm, vmem, hbm, vmem],
        out_specs=vmem,
        scratch_shapes=[
            pltpu.VMEM((SEGS, height, EPOCH_STEPS), jnp.int32),
            pltpu.VMEM((SEGS * EPOCH_STEPS, 3 * WIDTH), jnp.bfloat16),
            pltpu.VMEM((nr, height, WIDTH), jnp.bfloat16),
            pltpu.VMEM((nr, height, WIDTH), jnp.bfloat16),
            pltpu.VMEM((nr, 8, height), jnp.float32),
            pltpu.VMEM((nb, height, WIDTH), jnp.bfloat16),
            pltpu.VMEM((nb, MODES, height), jnp.bfloat16),
            pltpu.VMEM((nr, MODES, height), jnp.float32),
            pltpu.VMEM((nr, MODES, height), jnp.float32),
            pltpu.VMEM((nr * nb, MODES // 4, 4 * MODES), jnp.float32),
            dma((SEGS,)), dma,
            dma((nr,)), dma((nr,)),
            dma((nb,)), dma((nb,)), dma((nb,)), dma((nb,)),
            dma((nr,)), dma((nr,)),
            dma((nr * nb,)), dma((nr * nb,)),
        ],
        compiler_params=pltpu.CompilerParams(
            collective_id=0, has_side_effects=True, vmem_limit_bytes=40 * 1024 * 1024
        ),
        name="subspace_step",
    )(counts, subspace.T, jnp.asarray(split_table()), jnp.asarray(twist_matrix()))
    return modes_t.T


def solution(mesh):
    nr, nb = mesh.shape["row"], mesh.shape["blk"]
    return jax.shard_map(
        functools.partial(local, nr, nb),
        mesh=mesh,
        in_specs=(P(("freq", "row", "blk"), None, None), P(("freq", "row", "blk"), None)),
        out_specs=P(("freq", "row", "blk"), None),
        check_vma=False,
    )
```

time: 148 us -> 33.2 us (0.22)
  blocking collectives: 111 us -> 0 us
  Pallas kernels: 0 us -> 28.4 us
  between operations: 13.6 us -> 0.01 us
  other arithmetic: 11.4 us -> 0 us
  matrix products: 8.82 us -> 0 us
  local copies, waits for them, and re-layouts: 2.69 us -> 4.45 us
    psum x1 -> x0, blocking collectives: 59.6 us -> none  [local(): gram = lax.psum(local_gram, ('row', 'blk'))]
    all_gather x3 -> x0, blocking collectives: 51.6 us -> none  [the longest x1 38 us: local(): lax.all_gather(krylov_cluster, 'blk', axis=0, tiled=True)]
    pallas_call x0 -> x1, Pallas kernels: none -> 28.4 us  [local(): pl.pallas_call(functools.partial(kernel, nr, nb), out_shape=jax.ShapeDtyp...]
    dot_general x6 -> x0, matrix products: 7.96 us -> none  [the longest x2 3.51 us: tile_image(): lax.dot_general(stacked, column_spectra, (((1,), (1,)), ((), ())), prefer...]
    another operation x6 -> x0, other arithmetic: 6.69 us -> none  [the longest x3 3.59 us: local(): factor = jnp.linalg.cholesky(gram)]
    reduce_sum x4 -> x0, other arithmetic: 4.46 us -> none  [the longest x3 2.88 us: inverse_power(): return 1.0 / (jnp.sum(widened * widened, axis=1) + 1e-05)]
    unnamed x4 -> x9, local copies, waits for them, and re-layouts: 0.31 us -> 4.45 us
    convert_element_type x3 -> x0, local copies, waits for them, and re-layouts: 1.82 us -> none  [make_spectra(): return result.reshape(height, SEGS * 2 * TAPERS).astype(jnp.bfloat16)]
  transfers between devices with their start and end apart: 1 -> 0, of which waited for: 1 -> 0; matrix products, arithmetic and copies ran while one was open for 1% -> 0% of each run, Pallas kernels for 0% -> 0%
where the time goes in v1:
time: 33.2 us; the launch traced here: 32.9 us
  Pallas kernels  28.4 us (86%)
  local copies, waits for them, and re-layouts  4.45 us (13%)
    pallas_call x1, Pallas kernels, local(): pl.pallas_call(functools.partial(kernel, nr, nb), out_shape=jax.ShapeDtyp...  28.4 us
    unnamed x9, local copies, waits for them, and re-layouts  4.45 us

profile of v1, /device:TPU:0, one launch (start us, length us, event | category | flops | bytes accessed | tf_op | source)
XLA Modules:
  0.0 32.9 jit_solution(7988494819891539385)
XLA Ops:
  0.0 0.0 copy-start
  0.0 1.2 %copy-done = s32[256,8,128]{2,1,0:T(8,128)S(1)} copy-done((s32[256,8,128]{2,1,0:T(8,128)S(1)}, s32[256,8,128]{2,1,0:T(8,128)}, u32[]{:S(2)}) %copy-start) | copy-done | bytes 1048600
  1.2 0.0 copy-start.1
  1.2 1.1 %copy-done.1 = bf16[1024,384]{1,0:T(8,128)(2,1)S(1)} copy-done((bf16[1024,384]{1,0:T(8,128)(2,1)S(1)}, bf16[1024,384]{1,0:T(8,128)(2,1)}, u32[]{:S(2)}) %copy-start.1) | copy-done | bytes 786456
  2.4 0.0 copy-start.2
  2.4 0.8 %copy-done.2 = bf16[128,128]{1,0:T(8,128)(2,1)S(1)} copy-done((bf16[128,128]{1,0:T(8,128)(2,1)S(1)}, bf16[128,128]{1,0:T(8,128)(2,1)}, u32[]{:S(2)}) %copy-start.2) | copy-done | bytes 32792
  3.1 0.0 copy-start.3
  3.1 0.7 %copy-done.3 = bf16[256,32]{0,1:T(8,128)(2,1)S(1)} copy-done((bf16[256,32]{0,1:T(8,128)(2,1)S(1)}, bf16[256,32]{0,1:T(8,128)(2,1)}, u32[]{:S(2)}) %copy-start.3) | copy-done | bytes 16408
  3.8 28.4 %subspace_step.1 = f32[32,256]{1,0:T(8,128)S(1)} custom-call(s32[256,8,128]{2,1,0:T(8,128)S(1)} %copy-done, bf16[32,256]{1,0:T(8,128)(2,1)S(1)} %bitcast.3, bf16[1024,384]{1,0:T(8,128)(2,1)S(1)} %copy-done.1, bf16[128,128]{1,0:T(8,128)(2,1)S(1)} %copy-done.2), custom_call_target="tpu_custom_call" | custom-call | tf_op jit(solution)/shard_map/subspace_step/pallas_call | solution.py:220
  32.3 0.6 %copy.6 = f32[256,32]{0,1:T(8,128)} copy(f32[256,32]{0,1:T(8,128)S(1)} %bitcast.2) | data formatting | bytes 65536
Async XLA Ops:
  0.0 1.2 %copy-start = (s32[256,8,128]{2,1,0:T(8,128)S(1)}, s32[256,8,128]{2,1,0:T(8,128)}, u32[]{:S(2)}) copy-start(s32[256,8,128]{2,1,0:T(8,128)} %counts.1) | copy-start | bytes 3145732
  1.2 1.1 %copy-start.1 = (bf16[1024,384]{1,0:T(8,128)(2,1)S(1)}, bf16[1024,384]{1,0:T(8,128)(2,1)}, u32[]{:S(2)}) copy-start(bf16[1024,384]{1,0:T(8,128)(2,1)} %constant.4.clone.table) | copy-start | bytes 2359300
  2.4 0.8 %copy-start.2 = (bf16[128,128]{1,0:T(8,128)(2,1)S(1)}, bf16[128,128]{1,0:T(8,128)(2,1)}, u32[]{:S(2)}) copy-start(bf16[128,128]{1,0:T(8,128)(2,1)} %constant.5.clone.twist) | copy-start | bytes 98308
  3.1 0.7 %copy-start.3 = (bf16[256,32]{0,1:T(8,128)(2,1)S(1)}, bf16[256,32]{0,1:T(8,128)(2,1)}, u32[]{:S(2)}) copy-start(bf16[256,32]{0,1:T(8,128)(2,1)} %param.5) | copy-start | bytes 49156

commit v2 on v1

--- a/solution.py
+++ b/solution.py
@@ -45,13 +45,12 @@
 
 
 def twist_matrix():
-    m = np.zeros((WIDTH, WIDTH), np.float32)
-    for s in range(SEGS):
-        for c in range(TAPERS):
-            re, im = s * 2 * TAPERS + c, s * 2 * TAPERS + TAPERS + c
-            m[im, re] = 1.0
-            m[re, im] = -1.0
-    return m.astype(ml_dtypes.bfloat16)
+    source = lax.broadcasted_iota(jnp.int32, (WIDTH, WIDTH), 0)
+    target = lax.broadcasted_iota(jnp.int32, (WIDTH, WIDTH), 1)
+    real = lax.rem(target, 2 * TAPERS) < TAPERS
+    plus = jnp.where(real & (source == target + TAPERS), 1.0, 0.0)
+    minus = jnp.where(jnp.logical_not(real) & (source == target - TAPERS), 1.0, 0.0)
+    return (plus - minus).astype(jnp.bfloat16)
 
 
 def each(first, last, body):
@@ -69,9 +68,9 @@
 
 
 def kernel(
-    nr, nb, counts, sub_t, table, twist, out,
+    nr, nb, counts, sub_t, table, out,
     xs, tab, rows, twisted, irow, cols, subs, part, landed, grams,
-    x_sem, t_sem, row_send, row_recv, col_send, col_recv, sub_send, sub_recv,
+    x_sem, t_sem, s_sem, row_send, row_recv, col_send, col_recv, sub_send, sub_recv,
     part_send, part_recv, gram_send, gram_recv,
 ):
     my_row, my_blk = lax.axis_index("row"), lax.axis_index("blk")
@@ -80,17 +79,33 @@
     def peer(dr, db):
         return {"row": lax.rem(my_row + dr, nr), "blk": lax.rem(my_blk + db, nb)}
 
+    upper = (2 * my_blk) // nb
+    place = my_blk + upper * (nb - 1 - 2 * my_blk)
+
+    def near(j):
+        u = j + (j - place + nb) // nb
+        return u + upper * (nb - 1 - 2 * u)
+
+    def sent(j):
+        return lax.rem(near(j) - my_blk + nb, nb)
+
+    def taken(j):
+        return lax.rem(my_blk - near(j) + nb, nb)
+
+    barrier = pltpu.get_barrier_semaphore()
+    each(1, nb, lambda d: pl.semaphore_signal(
+        barrier, inc=1, device_id=peer(0, d), device_id_type=MESH))
+    each(1, nr, lambda d: pl.semaphore_signal(
+        barrier, inc=1, device_id=peer(d, 0), device_id_type=MESH))
+
     loads = [pltpu.make_async_copy(counts.at[:, s], xs.at[s], x_sem.at[s]) for s in range(SEGS)]
     table_load = pltpu.make_async_copy(table, tab, t_sem)
     table_load.start()
+    sub_load = pltpu.make_async_copy(sub_t, subs.at[0], s_sem)
+    sub_load.start()
     for load in loads:
         load.start()
 
-    barrier = pltpu.get_barrier_semaphore()
-    each(1, nr * nb, lambda k: pl.semaphore_signal(
-        barrier, inc=1, device_id=peer(k // nb, k % nb), device_id_type=MESH))
-
-    subs[0] = sub_t[...]
     table_load.wait()
     total = jnp.zeros((height, 3 * WIDTH), jnp.float32)
     for s in range(0, SEGS, 2):
@@ -105,7 +120,9 @@
     rows[0] = spectra
     cols[0] = spectra
 
-    pl.semaphore_wait(barrier, nr * nb - 1)
+    pl.semaphore_wait(barrier, nr + nb - 2)
+
+    sub_load.wait()
 
     def col_copy(d):
         return pltpu.make_async_remote_copy(
@@ -127,25 +144,27 @@
             src_ref=part.at[d], dst_ref=landed.at[d], send_sem=part_send.at[d],
             recv_sem=part_recv.at[d], device_id=peer(nr - d, 0), device_id_type=MESH)
 
-    def gram_copy(k):
+    def gram_copy(dr, db):
+        k = dr * nb + db
         return pltpu.make_async_remote_copy(
             src_ref=grams.at[0], dst_ref=grams.at[k], send_sem=gram_send.at[k],
-            recv_sem=gram_recv.at[k], device_id=peer(k // nb, k % nb), device_id_type=MESH)
-
+            recv_sem=gram_recv.at[k], device_id=peer(dr, db), device_id_type=MESH)
+
+    def send_cols(j):
+        d = sent(nb - 2 - j)
+        sub_copy(d).start()
+        col_copy(d).start()
+
+    each(0, nb - 1, send_cols)
     each(1, nr, lambda d: row_copy(d).start())
-
-    def send_cols(d):
-        col_copy(d).start()
-        sub_copy(d).start()
-
-    each(1, nb, send_cols)
 
     degrees = float(SEGS * TAPERS)
     ones = jnp.ones((8, WIDTH), jnp.float32)
+    twist = twist_matrix()
 
     def prepare_row(r):
         here = rows[r]
-        twisted[r] = jnp.dot(here, twist[...], preferred_element_type=jnp.float32).astype(jnp.bfloat16)
+        twisted[r] = jnp.dot(here, twist, preferred_element_type=jnp.float32).astype(jnp.bfloat16)
         wide = here.astype(jnp.float32)
         power = nt(ones, wide * wide, lax.Precision.HIGHEST)
         irow[r] = (degrees / (degrees - 1.0)) / (power + 1e-05)
@@ -165,32 +184,40 @@
     own = column(0)
     for r in range(nr):
         if r > 0:
-            row_copy(r).wait()
+            row_copy(r).wait_recv()
         prepare_row(r)
         part[r] = tile(0, r, own)
 
-    def add_column(d, final):
-        col_copy(d).wait()
-        sub_copy(d).wait()
+    def add_column(j, final):
+        d = taken(j)
+        sub_copy(d).wait_recv()
+        col_copy(d).wait_recv()
         icol = column(d)
         for r in list(range(1, nr)) + [0]:
             part[r] += tile(d, r, icol)
             if final and r > 0:
                 part_copy(r).start()
 
-    each(1, nb - 1, lambda d: add_column(d, False))
-    add_column(nb - 1, True)
+    each(0, nb - 2, lambda j: add_column(j, False))
+    add_column(nb - 2, True)
 
     image = part[0]
     for r in range(1, nr):
-        part_copy(r).wait()
+        part_copy(r).wait_recv()
         image += landed[r]
 
     gram = nt(image, image, lax.Precision.HIGHEST)
     quarter = MODES // 4
     grams[0] = jnp.concatenate([gram[q * quarter : (q + 1) * quarter] for q in range(4)], axis=1)
-    each(1, nr * nb, lambda k: gram_copy(k).start())
-    each(1, nr * nb, lambda k: gram_copy(k).wait())
+
+    def send_gram(j):
+        d = sent(nb - 2 - j)
+        for dr in range(nr):
+            gram_copy(dr, d).start()
+
+    each(0, nb - 1, send_gram)
+    each(1, nr, lambda d: gram_copy(d, 0).start())
+    each(1, nr * nb, lambda k: gram_copy(k // nb, k % nb).wait_recv())
     packed = jnp.sum(grams[...], axis=0)
     gram = jnp.concatenate([packed[:, q * MODES : (q + 1) * MODES] for q in range(4)], axis=0)
 
@@ -198,18 +225,34 @@
     lane_id = lax.broadcasted_iota(jnp.int32, (MODES, 2 * MODES), 1)
     eye = (sub_id == lane_id).astype(jnp.float32)
     work = jnp.concatenate([eye[:, :MODES], gram], axis=1)
-    for k in range(MODES - 1):
-        top = work[k : k + 1]
-        pivot = work[k : k + 1, MODES + k : MODES + k + 1]
-        below = work[:, MODES + k : MODES + k + 1]
-        update = below * (top * (1.0 / pivot))
-        work = work - jnp.where(sub_id > k, update, 0.0)
+    for k in range(0, MODES, 2):
+        c = MODES + k
+        first, second = work[k : k + 1], work[k + 1 : k + 2]
+        left, right = work[:, c : c + 1], work[:, c + 1 : c + 2]
+        scaled = first * (1.0 / work[k : k + 1, c : c + 1])
+        cross = scaled[:, c + 1 : c + 2]
+        second = second - scaled * work[k + 1 : k + 2, c : c + 1]
+        right = right - left * cross
+        second = second * (1.0 / second[:, c + 1 : c + 2])
+        work = work - jnp.where(sub_id > k, left, 0.0) * scaled - jnp.where(sub_id > k + 1, right, 0.0) * second
     pivots = jnp.sum(jnp.where(lane_id == sub_id + MODES, work, 0.0), axis=1, keepdims=True)
     neurons = float(height * nr * nb)
     inverse = work[:, :MODES] * (math.sqrt(neurons) / jnp.sqrt(pivots))
     out[...] = jnp.dot(
         inverse, image, precision=lax.Precision.HIGHEST, preferred_element_type=jnp.float32
     )
+
+    def sent_cols(d):
+        sub_copy(d).wait_send()
+        col_copy(d).wait_send()
+
+    def sent_rows(d):
+        row_copy(d).wait_send()
+        part_copy(d).wait_send()
+
+    each(1, nb, sent_cols)
+    each(1, nr, sent_rows)
+    each(1, nr * nb, lambda k: gram_copy(k // nb, k % nb).wait_send())
 
 
 def local(nr, nb, counts, subspace):
@@ -220,7 +263,7 @@
     modes_t = pl.pallas_call(
         functools.partial(kernel, nr, nb),
         out_shape=jax.ShapeDtypeStruct((MODES, height), jnp.float32),
-        in_specs=[hbm, vmem, hbm, vmem],
+        in_specs=[hbm, hbm, hbm],
         out_specs=vmem,
         scratch_shapes=[
             pltpu.VMEM((SEGS, height, EPOCH_STEPS), jnp.int32),
@@ -233,7 +276,7 @@
             pltpu.VMEM((nr, MODES, height), jnp.float32),
             pltpu.VMEM((nr, MODES, height), jnp.float32),
             pltpu.VMEM((nr * nb, MODES // 4, 4 * MODES), jnp.float32),
-            dma((SEGS,)), dma,
+            dma((SEGS,)), dma, dma,
             dma((nr,)), dma((nr,)),
             dma((nb,)), dma((nb,)), dma((nb,)), dma((nb,)),
             dma((nr,)), dma((nr,)),
@@ -243,7 +286,7 @@
             collective_id=0, has_side_effects=True, vmem_limit_bytes=40 * 1024 * 1024
         ),
         name="subspace_step",
-    )(counts, subspace.T, jnp.asarray(split_table()), jnp.asarray(twist_matrix()))
+    )(counts, subspace.T, jnp.asarray(split_table()))
     return modes_t.T
 
 

time: 33.2 us -> 31 us (0.934)
  Pallas kernels: 28.4 us -> 27.1 us
  local copies, waits for them, and re-layouts: 4.45 us -> 3.69 us
    pallas_call x1, Pallas kernels: 28.4 us -> 27.1 us  [local(): pl.pallas_call(functools.partial(kernel, nr, nb), out_shape=jax.ShapeDtyp...]
    unnamed x9 -> x7, local copies, waits for them, and re-layouts: 4.45 us -> 3.69 us
where the time goes in v2:
time: 31 us; the launch traced here: 30.8 us
  Pallas kernels  27.1 us (87%)
  local copies, waits for them, and re-layouts  3.69 us (12%)
    pallas_call x1, Pallas kernels, local(): pl.pallas_call(functools.partial(kernel, nr, nb), out_shape=jax.ShapeDtyp...  27.1 us
    unnamed x7, local copies, waits for them, and re-layouts  3.69 us

profile of v2, /device:TPU:0, one launch (start us, length us, event | category | flops | bytes accessed | tf_op | source)
XLA Modules:
  0.0 30.8 jit_solution(7970562577554556517)
XLA Ops:
  0.0 0.0 copy-start
  0.0 1.2 %copy-done = s32[256,8,128]{2,1,0:T(8,128)S(1)} copy-done((s32[256,8,128]{2,1,0:T(8,128)S(1)}, s32[256,8,128]{2,1,0:T(8,128)}, u32[]{:S(2)}) %copy-start) | copy-done | bytes 1048600
  1.2 0.0 copy-start.1
  1.2 1.1 %copy-done.1 = bf16[1024,384]{1,0:T(8,128)(2,1)S(1)} copy-done((bf16[1024,384]{1,0:T(8,128)(2,1)S(1)}, bf16[1024,384]{1,0:T(8,128)(2,1)}, u32[]{:S(2)}) %copy-start.1) | copy-done | bytes 786456
  2.4 0.0 copy-start.2
  2.4 0.7 %copy-done.2 = bf16[256,32]{0,1:T(8,128)(2,1)S(1)} copy-done((bf16[256,32]{0,1:T(8,128)(2,1)S(1)}, bf16[256,32]{0,1:T(8,128)(2,1)}, u32[]{:S(2)}) %copy-start.2) | copy-done | bytes 16408
  3.1 27.1 %subspace_step.1 = f32[32,256]{1,0:T(8,128)S(1)} custom-call(s32[256,8,128]{2,1,0:T(8,128)S(1)} %copy-done, bf16[32,256]{1,0:T(8,128)(2,1)S(1)} %bitcast.3, bf16[1024,384]{1,0:T(8,128)(2,1)S(1)} %copy-done.1), custom_call_target="tpu_custom_call" | custom-call | tf_op jit(solution)/shard_map/subspace_step/pallas_call | solution.py:263
  30.2 0.6 %copy.5 = f32[256,32]{0,1:T(8,128)} copy(f32[256,32]{0,1:T(8,128)S(1)} %bitcast.2) | data formatting | bytes 65536
Async XLA Ops:
  0.0 1.2 %copy-start = (s32[256,8,128]{2,1,0:T(8,128)S(1)}, s32[256,8,128]{2,1,0:T(8,128)}, u32[]{:S(2)}) copy-start(s32[256,8,128]{2,1,0:T(8,128)} %counts.1) | copy-start | bytes 3145732
  1.2 1.1 %copy-start.1 = (bf16[1024,384]{1,0:T(8,128)(2,1)S(1)}, bf16[1024,384]{1,0:T(8,128)(2,1)}, u32[]{:S(2)}) copy-start(bf16[1024,384]{1,0:T(8,128)(2,1)} %constant.2.clone.table) | copy-start | bytes 2359300
  2.4 0.7 %copy-start.2 = (bf16[256,32]{0,1:T(8,128)(2,1)S(1)}, bf16[256,32]{0,1:T(8,128)(2,1)}, u32[]{:S(2)}) copy-start(bf16[256,32]{0,1:T(8,128)(2,1)} %param.4) | copy-start | bytes 49156

commit v3 on v2

--- a/solution.py
+++ b/solution.py
@@ -283,7 +283,7 @@
             dma((nr * nb,)), dma((nr * nb,)),
         ],
         compiler_params=pltpu.CompilerParams(
-            collective_id=0, has_side_effects=True, vmem_limit_bytes=40 * 1024 * 1024
+            collective_id=0, has_side_effects=True, vmem_limit_bytes=58368 * 1024
         ),
         name="subspace_step",
     )(counts, subspace.T, jnp.asarray(split_table()))

time: 31 us -> 29.3 us (0.945)
  local copies, waits for them, and re-layouts: 3.69 us -> 1.38 us
  Pallas kernels: 27.1 us -> 27.7 us
    unnamed x7 -> x1, local copies, waits for them, and re-layouts: 3.69 us -> 1.38 us
    pallas_call x1, Pallas kernels: 27.1 us -> 27.7 us  [local(): pl.pallas_call(functools.partial(kernel, nr, nb), out_shape=jax.ShapeDtyp...]
where the time goes in v3:
time: 29.3 us; the launch traced here: 29.1 us
  Pallas kernels  27.7 us (95%)
  local copies, waits for them, and re-layouts  1.38 us (5%)
    pallas_call x1, Pallas kernels, local(): pl.pallas_call(functools.partial(kernel, nr, nb), out_shape=jax.ShapeDtyp...  27.7 us
    unnamed x1, local copies, waits for them, and re-layouts  1.38 us

profile of v3, /device:TPU:0, one launch (start us, length us, event | category | flops | bytes accessed | tf_op | source)
XLA Modules:
  0.0 29.1 jit_solution(5367550540953474956)
XLA Ops:
  0.0 27.7 %subspace_step.1 = f32[32,256]{1,0:T(8,128)} custom-call(s32[256,8,128]{2,1,0:T(8,128)} %counts.1, bf16[32,256]{1,0:T(8,128)(2,1)} %bitcast.3, bf16[1024,384]{1,0:T(8,128)(2,1)} %constant.2.clone.table), custom_call_target="tpu_custom_call" | custom-call | tf_op jit(solution)/shard_map/subspace_step/pallas_call | solution.py:263
  27.7 1.4 %copy.5 = f32[256,32]{0,1:T(8,128)} copy(f32[256,32]{0,1:T(8,128)} %bitcast.2) | data formatting | bytes 65536
